TPU v7x, 32 devices: a whole 2x2x4 slice. The times are simulated.
32 devices in a mesh: shot: 8 (over z, y), recv: 4 (over x, core).
Axes of the slice: x: 2, y: 2, z: 4, core: 2. Of those that a mesh axis runs over, the one named last changes fastest.
Arguments:
- traces: bfloat16 [2, 2, 4096, 4096], P(None, None, 'shot', 'recv'), may hold values from -6 to 6
Outputs:
- multiples: float32 [2, 2, 4096, 4096], P(None, None, 'shot', 'recv')
All inputs are finite; a program needn't handle non-finite values.
Results may differ from a plain program's by a relative error of at most 0.0044.
Values may be sent and summed in bfloat16 or wider, within the bound.
A program may use at most 128 MiB of HBM per device.

v0:
```python
import jax
import jax.numpy as jnp
from jax import lax
from jax.sharding import PartitionSpec as P

NS = 4096


def complex_product(left_block, right_block, form):
    real_real = jnp.einsum(
        form, left_block[:, 0], right_block[:, 0], preferred_element_type=jnp.float32
    )
    imag_imag = jnp.einsum(
        form, left_block[:, 1], right_block[:, 1], preferred_element_type=jnp.float32
    )
    real_imag = jnp.einsum(
        form, left_block[:, 0], right_block[:, 1], preferred_element_type=jnp.float32
    )
    imag_real = jnp.einsum(
        form, left_block[:, 1], right_block[:, 0], preferred_element_type=jnp.float32
    )
    return jnp.stack((real_real - imag_imag, real_imag + imag_real), axis=1)


def per_device(traces):
    freqs = traces.shape[0]
    block_rows = traces.shape[2]
    col_width = traces.shape[3]
    recv_count = lax.axis_size("recv")
    shot_count = lax.axis_size("shot")
    group_blocks = shot_count // recv_count
    piece_len = block_rows // recv_count
    total = shot_count * block_rows
    row_split = traces.reshape(freqs, 2, recv_count, piece_len, col_width)
    col_split = traces.reshape(freqs, 2, block_rows, group_blocks, recv_count, piece_len)
    col_split = jnp.transpose(col_split, (0, 1, 4, 2, 3, 5))
    got_rows, got_cols = (
        lax.all_to_all(row_split, "recv", split_axis=2, concat_axis=2, tiled=True),
        lax.all_to_all(col_split, "recv", split_axis=2, concat_axis=2, tiled=True),
    )
    wide_rows = jnp.transpose(got_rows, (0, 1, 3, 2, 4)).reshape(freqs, 2, piece_len, total)
    own_cols = jnp.transpose(got_cols, (0, 1, 3, 2, 4, 5)).reshape(freqs, 2, block_rows, col_width)
    mirrored = lax.all_to_all(wide_rows, "shot", split_axis=3, concat_axis=2, tiled=True)
    summed = own_cols.astype(jnp.float32) + jnp.swapaxes(mirrored, 2, 3).astype(jnp.float32)
    averaged = (summed * 0.5).astype(jnp.bfloat16)
    spread = lax.all_gather(averaged, "recv", axis=3, tiled=True)
    spread = spread.reshape(freqs, 2, block_rows, recv_count, shot_count, piece_len)
    panel = jnp.transpose(spread, (0, 1, 2, 4, 3, 5)).reshape(freqs, 2, block_rows, total)
    recv_index = lax.axis_index("recv")
    own_tile = lax.dynamic_slice_in_dim(panel, recv_index * col_width, col_width, 3)
    product = complex_product(
        panel, lax.all_gather(own_tile, "shot", axis=2, tiled=True), "fik,fkj->fij"
    )
    scale_factor = jnp.float32(float(NS) ** (-0.5))
    return product * scale_factor


def solution(mesh):
    placed = (P(None, None, "shot", "recv"),)
    return jax.shard_map(
        per_device,
        mesh=mesh,
        in_specs=placed,
        out_specs=P(None, None, "shot", "recv"),
        check_vma=False,
    )
```

profile of v0, /device:TPU:24, one launch (start us, length us, event | category | flops | bytes accessed | tf_op | source)
XLA Modules:
  0.0 1126.6 jit_solution(12019277324089544270)
XLA Ops:
  6.5 4.8 copy.15
  11.3 4.8 all-to-all-start.1
  16.2 6.2 copy.12
  22.4 4.6 copy.13
  27.0 37.4 %all-to-all-done.1 = bf16[2,2,4,128,1024]{4,3,1,0,2:T(8,128)(2,1)} async-done(((bf16[2,2,4,128,1024]{4,3,1,0,2:T(8,128)(2,1)}), bf16[2,2,4,128,1024]{4,3,1,0,2:T(8,128)(2,1)}, u32[]{:S(2)}, u32[]{:S(2)}) %all-to-all-start.1) | async-done | bytes 4194336 | tf_op jit(solution)/shard_map/all_to_all | solution.py:38
  64.4 4.9 all-to-all-start
  69.4 6.2 copy.16
  75.6 10.1 copy.17
  85.7 31.9 %all-to-all-done = bf16[2,2,4,512,2,128]{3,5,4,1,0,2:T(8,128)(2,1)} async-done(((bf16[2,2,4,512,2,128]{3,5,4,1,0,2:T(8,128)(2,1)}), bf16[2,2,4,512,2,128]{3,5,4,1,0,2:T(8,128)(2,1)}, u32[]{:S(2)}, u32[]{:S(2)}) %all-to-all-start) | async-done | bytes 4194336 | tf_op jit(solution)/shard_map/all_to_all | solution.py:39
  117.6 6.1 all-to-all-start.2
  123.6 0.0 all-gather.3.cloned.1.call-start
  123.6 6.5 copy_convert_fusion
  130.2 85.0 %all-to-all-done.2 = bf16[2,2,128,4096]{2,1,0,3:T(2,128)(2,1)} async-done(((bf16[2,2,128,4096]{2,1,0,3:T(2,128)(2,1)}), bf16[2,2,128,4096]{2,1,0,3:T(2,128)(2,1)}, u32[]{:S(2)}, u32[]{:S(2)}) %all-to-all-start.2) | async-done | bytes 4194336 | tf_op jit(solution)/shard_map/all_to_all | solution.py:43
  215.2 2.7 copy.18
  217.9 4.4 convert_bitcast_fusion
  222.3 8.7 copy.19
  231.0 10.0 fusion.5
  241.0 0.0 all-gather.3.cloned.1.call-update
  241.0 0.2 all-gather.5.cloned.1.call-start
  241.3 105.1 %all-gather.3.cloned.1.call-done = bf16[2,2,512,4096]{2,3,1,0:T(8,128)(2,1)} async-done(((bf16[2,2,512,1024]{2,3,1,0:T(8,128)(2,1)}), bf16[2,2,512,4096]{2,3,1,0:T(8,128)(2,1)}) %all-gather.3.cloned.1.call-update) | async-done | bytes 16777232 | tf_op jit(solution)/shard_map/all_gather | solution.py:46
  346.4 28.6 %copy.20 = bf16[2,2,512,8,4,128]{5,4,3,2,0,1:T(4,128)(2,1)} copy(bf16[2,2,512,8,4,128]{2,5,3,4,1,0:T(8,128)(2,1)} %bitcast.57) | data formatting | bytes 33554432 | tf_op jit(solution)/shard_map/transpose | solution.py:48
  375.0 27.7 %reshape.26 = bf16[2,2,512,4096]{3,2,0,1:T(8,128)(2,1)} reshape(bf16[2,2,512,8,4,128]{5,4,3,2,0,1:T(4,128)(2,1)} %copy.20) | data formatting | bytes 33554432 | tf_op jit(solution)/shard_map/reshape | solution.py:48
  402.7 4.6 constant_dynamic-slice_fusion
  407.3 0.0 all-gather.5.cloned.1.call-update
  407.3 637.9 %all-gather.5.cloned.1.call-done = bf16[2,2,4096,1024]{3,2,0,1:T(8,128)(2,1)} async-done(((bf16[2,2,512,1024]{3,2,0,1:T(8,128)(2,1)}), bf16[2,2,4096,1024]{3,2,0,1:T(8,128)(2,1)}) %all-gather.5.cloned.1.call-update) | async-done | bytes 33554448 | tf_op jit(solution)/shard_map/all_gather | solution.py:52
  1045.2 16.1 %fusion = f32[2,512,1024]{2,1,0:T(8,128)} fusion(bf16[2,2,4096,1024]{3,2,0,1:T(8,128)(2,1)} %all-gather.5.cloned.1.call-done, bf16[2,2,512,4096]{3,2,0,1:T(8,128)(2,1)} %reshape.26), kind=kOutput, calls=%fused_computation.2 | convolution fusion | flops 8589934592 | bytes 29360128 | tf_op jit(solution)/shard_map/fik,fkj->fij/dot_general | solution.py:19
  1061.3 16.2 %fusion.1 = f32[2,512,1024]{2,1,0:T(8,128)} fusion(bf16[2,2,4096,1024]{3,2,0,1:T(8,128)(2,1)} %all-gather.5.cloned.1.call-done, bf16[2,2,512,4096]{3,2,0,1:T(8,128)(2,1)} %reshape.26), kind=kOutput, calls=%fused_computation.3 | convolution fusion | flops 8589934592 | bytes 29360128 | tf_op jit(solution)/shard_map/fik,fkj->fij/dot_general | solution.py:10
  1077.5 16.7 %add_bitcast_fusion = f32[2,1,512,1024]{3,2,0,1:T(8,128)} fusion(f32[2,512,1024]{2,1,0:T(8,128)} %fusion, bf16[2,2,4096,1024]{3,2,0,1:T(8,128)(2,1)} %all-gather.5.cloned.1.call-done, bf16[2,2,512,4096]{3,2,0,1:T(8,128)(2,1)} %reshape.26), kind=kOutput, calls=%fused_computation.14 | convolution fusion | flops 8590983168 | bytes 33554432 | tf_op jit(solution)/shard_map/fik,fkj->fij/dot_general | solution.py:16
  1094.2 16.9 %subtract_bitcast_fusion = f32[2,1,512,1024]{3,2,0,1:T(8,128)} fusion(f32[2,512,1024]{2,1,0:T(8,128)} %fusion.1, bf16[2,2,4096,1024]{3,2,0,1:T(8,128)(2,1)} %all-gather.5.cloned.1.call-done, bf16[2,2,512,4096]{3,2,0,1:T(8,128)(2,1)} %reshape.26), kind=kOutput, calls=%fused_computation.15 | convolution fusion | flops 8590983168 | bytes 33554432 | tf_op jit(solution)/shard_map/fik,fkj->fij/dot_general | solution.py:13
  1111.0 4.4 maximum_multiply_fusion
  1115.5 4.2 copy.21
Async XLA Ops:
  11.3 53.1 %all-to-all-start.1 = ((bf16[2,2,4,128,1024]{4,3,1,0,2:T(8,128)(2,1)}), bf16[2,2,4,128,1024]{4,3,1,0,2:T(8,128)(2,1)}, u32[]{:S(2)}, u32[]{:S(2)}) async-start(bf16[2,2,4,128,1024]{4,3,1,0,2:T(8,128)(2,1)} %copy.15), calls=%async_computation.1 | async-start | bytes 8388608 | tf_op jit(solution)/shard_map/all_to_all | solution.py:38
  64.4 53.2 %all-to-all-start = ((bf16[2,2,4,512,2,128]{3,5,4,1,0,2:T(8,128)(2,1)}), bf16[2,2,4,512,2,128]{3,5,4,1,0,2:T(8,128)(2,1)}, u32[]{:S(2)}, u32[]{:S(2)}) async-start(bf16[2,2,4,512,2,128]{3,5,4,1,0,2:T(8,128)(2,1)} %copy.13), calls=%async_computation | async-start | bytes 8388608 | tf_op jit(solution)/shard_map/all_to_all | solution.py:39
  117.6 97.6 %all-to-all-start.2 = ((bf16[2,2,128,4096]{2,1,0,3:T(2,128)(2,1)}), bf16[2,2,128,4096]{2,1,0,3:T(2,128)(2,1)}, u32[]{:S(2)}, u32[]{:S(2)}) async-start(bf16[2,2,128,4096]{2,1,0,3:T(2,128)(2,1)} %copy.17), calls=%async_computation.2 | async-start | bytes 8388608 | tf_op jit(solution)/shard_map/all_to_all | solution.py:43
  123.6 222.7 %all-gather.3.cloned.1.call-start = ((), (), s32[]{:S(2)}) async-start(), calls=%async_computation.3 | async-start | bytes 20971520 | tf_op jit(solution)/shard_map/all_gather | solution.py:46
  241.0 804.2 %all-gather.5.cloned.1.call-start = ((), (), s32[]{:S(2)}) async-start(), calls=%async_computation.4 | async-start | bytes 37748736 | tf_op jit(solution)/shard_map/all_gather | solution.py:52
Sparse Core Ops, SparseCore 0:
  241.2 105.1 all-gather.2
  407.5 637.6 all-gather.4
where the time goes:
time: 1130 us
  waiting for transfers between devices  897 us (79%)
  local copies, waits for them, and re-layouts  109 us (10%)
  matrix products  65.8 us (6%)
  other arithmetic  25.4 us (2%)
  starting transfers between devices  16 us (1%)
  between operations  13.4 us (1%)
    all_gather x1, waiting for transfers between devices, per_device(): lax.all_gather(own_tile, 'shot', axis=2, tiled=True)  638 us
    all_gather x1, waiting for transfers between devices, per_device(): spread = lax.all_gather(averaged, 'recv', axis=3, tiled=True)  105 us
    all_to_all x1, waiting for transfers between devices, per_device(): lax.all_to_all(wide_rows, 'shot', split_axis=3, concat_axis=2, tiled=True)  85 us
    all_to_all x1, waiting for transfers between devices, per_device(): lax.all_to_all(row_split, 'recv', split_axis=2, concat_axis=2, tiled=True)  37.4 us
    all_to_all x1, waiting for transfers between devices, per_device(): lax.all_to_all(col_split, 'recv', split_axis=2, concat_axis=2, tiled=True)  31.9 us
    transpose x1, local copies, waits for them, and re-layouts, per_device(): jnp.transpose(spread, (0, 1, 2, 4, 3, 5))  28.6 us
    reshape x1, local copies, waits for them, and re-layouts, per_device(): jnp.transpose(spread, (0, 1, 2, 4, 3, 5))  27.7 us
  transfers between devices with their start and end apart: 5, of which 5 were waited for; matrix products, arithmetic and copies ran while one was open for 3% of the time, Pallas kernels for 0%

commit v1 on v0

--- a/solution.py
+++ b/solution.py
@@ -1,9 +1,275 @@
+import functools
+
 import jax
 import jax.numpy as jnp
 from jax import lax
+from jax.experimental import pallas as pl
+from jax.experimental.pallas import tpu as pltpu
 from jax.sharding import PartitionSpec as P
 
 NS = 4096
+MESH = pl.DeviceIdType.MESH
+ANY = pl.BlockSpec(memory_space=pl.ANY)
+
+
+class Place:
+    def __init__(self):
+        shot, recv = lax.axis_index("shot"), lax.axis_index("recv")
+        self.hi, self.zl, self.y = shot // 4, (shot // 2) % 2, shot % 2
+        self.x, self.core = recv // 2, recv % 2
+        self.row_group = self.zl * 2 + self.y
+        self.recv = recv
+
+    def device(self, **moved):
+        at = dict(hi=self.hi, zl=self.zl, y=self.y, x=self.x, core=self.core)
+        at.update(moved)
+        return ((at["hi"] * 2 + at["zl"]) * 2 + at["y"], at["x"] * 2 + at["core"])
+
+
+def greet(targets):
+    barrier = pltpu.get_barrier_semaphore()
+    for target in targets:
+        pl.semaphore_signal(barrier, inc=1, device_id=target, device_id_type=MESH)
+    pl.semaphore_wait(barrier, len(targets))
+
+
+def exchange_kernel(traces, tile, mirror, local_sems, swap_sems, send_sems, recv_sems):
+    me = Place()
+    size = traces.shape[2]
+    partner = me.device(hi=1 - me.hi)
+    blocks = [(flip, col) for flip in range(2) for col in range(2)]
+
+    def half(flip):
+        return me.hi if flip == 0 else 1 - me.hi
+
+    def target(flip, col):
+        return me.device(zl=me.core, y=col, x=half(flip), core=me.zl)
+
+    def is_self(flip, col):
+        return (me.core == me.zl) & (me.y == col) & (me.x == half(flip))
+
+    barrier = pltpu.get_barrier_semaphore()
+    pl.semaphore_signal(barrier, inc=1, device_id=partner, device_id_type=MESH)
+    for flip, col in blocks:
+        @pl.when(jnp.logical_not(is_self(flip, col)))
+        def _():
+            pl.semaphore_signal(barrier, inc=1, device_id=target(flip, col), device_id_type=MESH)
+    self_count = jnp.where((me.core == me.zl), 1, 0)
+    pl.semaphore_wait(barrier, 5 - self_count)
+
+    swaps = [
+        pltpu.make_async_remote_copy(
+            src_ref=traces.at[1 - me.hi, c], dst_ref=tile.at[c, me.hi],
+            send_sem=swap_sems.at[0, c], recv_sem=swap_sems.at[1, c],
+            device_id=partner, device_id_type=MESH,
+        )
+        for c in range(2)
+    ]
+    for swap in swaps:
+        swap.start()
+    own = pltpu.make_async_copy(traces.at[me.hi], tile.at[:, me.hi], local_sems.at[0])
+    own.start()
+
+    def source(flip, col, c):
+        columns = pl.ds(col * size, size)
+        if flip == 0:
+            return traces.at[me.hi, c, :, columns]
+        return tile.at[c, 1 - me.hi, :, columns]
+
+    def remote(flip, col, c):
+        return pltpu.make_async_remote_copy(
+            src_ref=source(flip, col, c), dst_ref=mirror.at[c, me.x, me.y],
+            send_sem=send_sems.at[c, half(flip), col], recv_sem=recv_sems.at[c, me.x, me.y],
+            device_id=target(flip, col), device_id_type=MESH,
+        )
+
+    def local(flip, col, c):
+        return pltpu.make_async_copy(
+            source(flip, col, c), mirror.at[c, me.x, me.y], local_sems.at[1 + c]
+        )
+
+    def begin(flip, c):
+        for col in range(2):
+            @pl.when(is_self(flip, col))
+            def _():
+                local(flip, col, c).start()
+
+            @pl.when(jnp.logical_not(is_self(flip, col)))
+            def _():
+                remote(flip, col, c).start()
+
+    for c in range(2):
+        begin(0, c)
+    for c in range(2):
+        swaps[c].wait_recv()
+        begin(1, c)
+    own.wait()
+    for c in range(2):
+        swaps[c].wait_send()
+        for flip, col in blocks:
+            @pl.when(is_self(flip, col))
+            def _():
+                local(flip, col, c).wait()
+
+            @pl.when(jnp.logical_not(is_self(flip, col)))
+            def _():
+                remote(flip, col, c).wait_send()
+                pltpu.make_async_remote_copy(
+                    src_ref=mirror.at[c, half(flip), col], dst_ref=mirror.at[c, half(flip), col],
+                    send_sem=send_sems.at[c, half(flip), col],
+                    recv_sem=recv_sems.at[c, half(flip), col],
+                    device_id=target(flip, col), device_id_type=MESH,
+                ).wait_recv()
+
+
+def exchange(traces):
+    size, width = traces.shape[2:]
+    return pl.pallas_call(
+        exchange_kernel,
+        out_shape=(
+            jax.ShapeDtypeStruct((2, 2, size, width), traces.dtype),
+            jax.ShapeDtypeStruct((2, 2, 2, size, width // 2), traces.dtype),
+        ),
+        in_specs=[ANY],
+        out_specs=(ANY, ANY),
+        scratch_shapes=[
+            pltpu.SemaphoreType.DMA((3,)),
+            pltpu.SemaphoreType.DMA((2, 2)),
+            pltpu.SemaphoreType.DMA((2, 2, 2)),
+            pltpu.SemaphoreType.DMA((2, 2, 2)),
+        ],
+        compiler_params=pltpu.CompilerParams(collective_id=0, has_side_effects=True),
+        name="exchange",
+    )(traces)
+
+
+def average_kernel(tile, mirror, out):
+    total = tile[0, 0].astype(jnp.float32) + jnp.transpose(mirror[0, 0, 0]).astype(jnp.float32)
+    out[0] = (total * 0.5).astype(out.dtype)
+
+
+def average(tile, mirror):
+    size, width = tile.shape[2:]
+    return pl.pallas_call(
+        average_kernel,
+        grid=(2, 2, 2),
+        out_shape=jax.ShapeDtypeStruct((2, 2 * size, width), tile.dtype),
+        in_specs=[
+            pl.BlockSpec((1, 1, size, size), lambda c, h, y: (c, h, 0, y)),
+            pl.BlockSpec((1, 1, 1, size, size), lambda c, h, y: (c, h, y, 0, 0)),
+        ],
+        out_specs=pl.BlockSpec((1, size, size), lambda c, h, y: (c, h, y)),
+        compiler_params=pltpu.CompilerParams(vmem_limit_bytes=32 * 2**20),
+        name="average",
+    )(tile, mirror)
+
+
+def gather_kernel(mean, rows, cols, local_sems, send_sems, recv_sems):
+    me = Place()
+    across_x, across_core = me.device(x=1 - me.x), me.device(core=1 - me.core)
+    across_y, across_z = me.device(y=1 - me.y), me.device(zl=1 - me.zl)
+    greet([across_x, across_core, across_y, across_z])
+    mine, group = me.recv, me.row_group
+    group_y = me.zl * 2 + 1 - me.y
+    group_z = (1 - me.zl) * 2 + me.y
+    recv_x = (1 - me.x) * 2 + me.core
+
+    def send(k, source, dest, device):
+        return pltpu.make_async_remote_copy(
+            src_ref=source, dst_ref=dest, send_sem=send_sems.at[k], recv_sem=recv_sems.at[k],
+            device_id=device, device_id_type=MESH,
+        )
+
+    copies = [
+        send(0, mean.at[0], cols.at[group, 0], across_y),
+        send(1, mean.at[1], cols.at[group, 1], across_z),
+        send(2, mean, rows.at[mine], across_x),
+        send(3, mean, rows.at[mine], across_core),
+        send(4, mean.at[1], cols.at[group, 1], across_y),
+        send(5, mean.at[0], cols.at[group, 0], across_z),
+    ]
+    relays = [
+        send(6, cols.at[group_y, 0], cols.at[group_y, 0], across_z),
+        send(7, cols.at[group_z, 1], cols.at[group_z, 1], across_y),
+        send(8, rows.at[recv_x], rows.at[recv_x], across_core),
+    ]
+    locals_ = [
+        pltpu.make_async_copy(mean, cols.at[group], local_sems.at[0]),
+        pltpu.make_async_copy(mean, rows.at[mine], local_sems.at[1]),
+    ]
+    for copy in copies + locals_:
+        copy.start()
+    for copy, relay in zip(copies, relays):
+        copy.wait_recv()
+        relay.start()
+    for copy in copies[3:] + relays:
+        copy.wait_recv()
+    for copy in copies + relays:
+        copy.wait_send()
+    for copy in locals_:
+        copy.wait()
+
+
+def gather(mean):
+    panel = jax.ShapeDtypeStruct((4,) + mean.shape, mean.dtype)
+    return pl.pallas_call(
+        gather_kernel,
+        out_shape=(panel, panel),
+        in_specs=[ANY],
+        out_specs=(ANY, ANY),
+        scratch_shapes=[
+            pltpu.SemaphoreType.DMA((2,)),
+            pltpu.SemaphoreType.DMA((9,)),
+            pltpu.SemaphoreType.DMA((9,)),
+        ],
+        compiler_params=pltpu.CompilerParams(collective_id=1, has_side_effects=True),
+        name="gather",
+    )(mean)
+
+
+def product_kernel(scale, rows, cols, out):
+    half = rows.shape[2] // 2
+    real = imag = None
+    for k in range(8):
+        left = rows.at[k // 2, :, :, pl.ds((k % 2) * half, half)]
+        right = cols.at[k % 4, :, pl.ds((k // 4) * half, half), :]
+        dot = functools.partial(jnp.dot, preferred_element_type=jnp.float32)
+        re = dot(left[0], right[0]) - dot(left[1], right[1])
+        im = dot(left[0], right[1]) + dot(left[1], right[0])
+        real, imag = (re, im) if real is None else (real + re, imag + im)
+    out[0] = real * scale
+    out[1] = imag * scale
+
+
+def product(rows, cols, tile_cols=256):
+    size = rows.shape[2]
+    return pl.pallas_call(
+        functools.partial(product_kernel, float(NS) ** (-0.5)),
+        grid=(size // tile_cols,),
+        out_shape=jax.ShapeDtypeStruct((2, size, size), jnp.float32),
+        in_specs=[
+            pl.BlockSpec(rows.shape, lambda n: (0, 0, 0, 0), pipeline_mode=pl.Buffered(1)),
+            pl.BlockSpec((4, 2, size, tile_cols), lambda n: (0, 0, 0, n)),
+        ],
+        out_specs=pl.BlockSpec((2, size, tile_cols), lambda n: (0, 0, n)),
+        compiler_params=pltpu.CompilerParams(vmem_limit_bytes=56 * 2**20),
+        cost_estimate=pl.CostEstimate(
+            flops=2 * 4 * size * size * 4 * size, bytes_accessed=40 * 2**20, transcendentals=0
+        ),
+        name="product",
+    )(rows, cols)
+
+
+def cube_per_device(traces):
+    size = traces.shape[2]
+    hi = lax.axis_index("shot") // 4
+    mean = average(*exchange(traces))
+    result = product(*gather(mean)).reshape(2, 2, size, 2 * size)
+    kept = lax.dynamic_index_in_dim(result, hi, 1, keepdims=False)
+    sent = lax.dynamic_index_in_dim(result, 1 - hi, 1, keepdims=False).astype(jnp.bfloat16)
+    got = lax.ppermute(sent, "shot", [(s, (s + 4) % 8) for s in range(8)]).astype(jnp.float32)
+    first = hi == 0
+    return jnp.stack((jnp.where(first, kept, got), jnp.where(first, got, kept)))
 
 
 def complex_product(left_block, right_block, form):
@@ -57,8 +323,9 @@
 
 def solution(mesh):
     placed = (P(None, None, "shot", "recv"),)
+    fits = mesh.shape["shot"] == 8 and mesh.shape["recv"] == 4
     return jax.shard_map(
-        per_device,
+        cube_per_device if fits else per_device,
         mesh=mesh,
         in_specs=placed,
         out_specs=P(None, None, "shot", "recv"),

time: 1130 us -> 536 us (0.47)
  waiting for transfers between devices: 897 us -> 91.6 us
  Pallas kernels: 0 us -> 419 us
  local copies, waits for them, and re-layouts: 109 us -> 8.89 us
  matrix products: 65.8 us -> 0 us
  other arithmetic: 25.4 us -> 8.23 us
  starting transfers between devices: 16 us -> 2.58 us
  between operations: 13.4 us -> 0.07 us
    all_gather x2 -> x0, waiting for transfers between devices: 743 us -> none  [the longest x1 638 us: per_device(): lax.all_gather(own_tile, 'shot', axis=2, tiled=True)]
    pallas_call x0 -> x4, Pallas kernels: none -> 419 us  [the longest x1 262 us: gather(): pl.pallas_call(gather_kernel, out_shape=(panel, panel), in_specs=[ANY], o...]
    all_to_all x3 -> x0, waiting for transfers between devices: 154 us -> none  [the longest x1 85 us: per_device(): lax.all_to_all(wide_rows, 'shot', split_axis=3, concat_axis=2, tiled=True)]
    ppermute x0 -> x1, waiting for transfers between devices: none -> 91.6 us  [cube_per_device(): lax.ppermute(sent, 'shot', [(s, (s + 4) % 8) for s in range(8)])]
    dot_general x4 -> x0, matrix products: 65.8 us -> none  [the longest x1 16.9 us: complex_product(): jnp.einsum(form, left_block[:, 1], right_block[:, 1], preferred_element_t...]
    reshape x3 -> x0, local copies, waits for them, and re-layouts: 42.6 us -> none  [the longest x1 27.7 us: per_device(): jnp.transpose(spread, (0, 1, 2, 4, 3, 5))]
    transpose x2 -> x0, local copies, waits for them, and re-layouts: 33.2 us -> none  [the longest x1 28.6 us: per_device(): jnp.transpose(spread, (0, 1, 2, 4, 3, 5))]
    convert_element_type x3 -> x0, other arithmetic: 21 us -> none  [the longest x1 10 us: per_device(): averaged = (summed * 0.5).astype(jnp.bfloat16)]
  transfers between devices with their start and end apart: 5 -> 1, of which waited for: 5 -> 1; matrix products, arithmetic and copies ran while one was open for 3% -> 0% of each run, Pallas kernels for 0% -> 0%
where the time goes in v1:
time: 536 us; the launch traced here: 530 us
  Pallas kernels  419 us (78%)
  waiting for transfers between devices  91.6 us (17%)
  local copies, waits for them, and re-layouts  8.89 us (2%)
  other arithmetic  8.23 us (2%)
    pallas_call x1, Pallas kernels, gather(): pl.pallas_call(gather_kernel, out_shape=(panel, panel), in_specs=[ANY], o...  262 us
    pallas_call x1, Pallas kernels, exchange(): pl.pallas_call(exchange_kernel, out_shape=(jax.ShapeDtypeStruct((2, 2, si...  111 us
    ppermute x1, waiting for transfers between devices, cube_per_device(): lax.ppermute(sent, 'shot', [(s, (s + 4) % 8) for s in range(8)])  91.6 us
    pallas_call x1, Pallas kernels, product(): pl.pallas_call(functools.partial(product_kernel, float(NS) ** (-0.5)), gr...  43.9 us
  transfers between devices with their start and end apart: 1, of which 1 were waited for; matrix products, arithmetic and copies ran while one was open for 0% of the time, Pallas kernels for 0%

profile of v1, /device:TPU:24, one launch (start us, length us, event | category | flops | bytes accessed | tf_op | source)
XLA Modules:
  0.0 530.3 jit_solution(8075317942963310435)
XLA Ops:
  0.0 110.9 %exchange.1 = (bf16[2,2,512,1024]{3,2,1,0:T(8,128)(2,1)}, bf16[2,2,2,512,512]{4,3,2,1,0:T(8,128)(2,1)}) custom-call(bf16[2,2,512,1024]{3,2,1,0:T(8,128)(2,1)} %traces.1), custom_call_target="tpu_custom_call" | custom-call | tf_op jit(solution)/shard_map/exchange/pallas_call | solution.py:127
  110.9 0.0 copy-start.1
  110.9 2.2 copy-done.1
  113.0 0.0 copy-start.2
  113.1 2.2 copy-done.2
  115.2 2.6 average.1.mean
  117.8 0.0 copy-start
  117.8 2.0 copy-done
  119.8 261.6 %gather.1 = (bf16[4,2,1024,1024]{3,2,1,0:T(8,128)(2,1)}, bf16[4,2,1024,1024]{3,2,1,0:T(8,128)(2,1)}) custom-call(bf16[2,1024,1024]{2,1,0:T(8,128)(2,1)} %copy-done), custom_call_target="tpu_custom_call" | custom-call | tf_op jit(solution)/shard_map/gather/pallas_call | solution.py:215
  381.4 43.9 %product.1 = f32[2,1024,1024]{2,1,0:T(8,128)} custom-call(bf16[4,2,1024,1024]{3,2,1,0:T(8,128)(2,1)} %get-tuple-element.11.rows, bf16[4,2,1024,1024]{3,2,1,0:T(8,128)(2,1)} %get-tuple-element.12.cols), custom_call_target="tpu_custom_call" | custom-call | flops 34359738368 | bytes 41943040 | tf_op jit(solution)/shard_map/product/pallas_call | solution.py:246
  425.3 2.5 fusion.2
  427.8 2.6 collective-permute-start
  430.4 91.6 %collective-permute-done = bf16[2,512,1024]{2,1,0:T(8,128)(2,1)} collective-permute-done((bf16[2,512,1024]{2,1,0:T(8,128)(2,1)S(1)}, bf16[2,512,1024]{2,1,0:T(8,128)(2,1)}, u32[]{:S(2)}, u32[]{:S(2)}) %collective-permute-start) | collective-permute-done | bytes 2097184 | tf_op jit(solution)/shard_map/ppermute | solution.py:270
  522.0 4.0 fusion
  526.0 4.2 pad_maximum_fusion
Async XLA Ops:
  110.9 2.2 copy-start.1
  113.0 2.2 copy-start.2
  117.8 2.0 copy-start
  427.8 94.2 %collective-permute-start = (bf16[2,512,1024]{2,1,0:T(8,128)(2,1)S(1)}, bf16[2,512,1024]{2,1,0:T(8,128)(2,1)}, u32[]{:S(2)}, u32[]{:S(2)}) collective-permute-start(bf16[2,512,1024]{2,1,0:T(8,128)(2,1)S(1)} %fusion.2), channel_id=1, source_target_pairs={{0,16},{4,20},{8,24},{12,28},{16,0},{20,4},{24,8},{28,12},{1,17},{... | collective-permute-start | bytes 6291464 | tf_op jit(solution)/shard_map/ppermute | solution.py:270

commit v2 on v1

--- a/solution.py
+++ b/solution.py
@@ -164,111 +164,182 @@
     )(tile, mirror)
 
 
-def gather_kernel(mean, rows, cols, local_sems, send_sems, recv_sems):
+def multiply_kernel(chunks, scale, mean, kept, got, rows, cols, home, acc, local_sems, send_sems, recv_sems):
     me = Place()
+    size = mean.shape[1] // 2
+    width = mean.shape[2]
+    wide = width // chunks
     across_x, across_core = me.device(x=1 - me.x), me.device(core=1 - me.core)
     across_y, across_z = me.device(y=1 - me.y), me.device(zl=1 - me.zl)
-    greet([across_x, across_core, across_y, across_z])
+    partner = me.device(hi=1 - me.hi)
+    greet([across_x, across_core, across_y, across_z, partner])
     mine, group = me.recv, me.row_group
     group_y = me.zl * 2 + 1 - me.y
     group_z = (1 - me.zl) * 2 + me.y
     recv_x = (1 - me.x) * 2 + me.core
-
-    def send(k, source, dest, device):
+    count = [0]
+
+    def remote(source, dest, device):
+        k = count[0]
+        count[0] += 1
         return pltpu.make_async_remote_copy(
             src_ref=source, dst_ref=dest, send_sem=send_sems.at[k], recv_sem=recv_sems.at[k],
             device_id=device, device_id_type=MESH,
         )
 
-    copies = [
-        send(0, mean.at[0], cols.at[group, 0], across_y),
-        send(1, mean.at[1], cols.at[group, 1], across_z),
-        send(2, mean, rows.at[mine], across_x),
-        send(3, mean, rows.at[mine], across_core),
-        send(4, mean.at[1], cols.at[group, 1], across_y),
-        send(5, mean.at[0], cols.at[group, 0], across_z),
+    def half(flip):
+        return pl.ds(pl.multiple_of((1 - me.hi if flip == 0 else me.hi) * size, size), size)
+
+    def part(j):
+        return pl.ds(j * wide, wide)
+
+    started = []
+
+    def start(*copies):
+        for copy in copies:
+            copy.start()
+            started.append(copy)
+
+    def arrive(*copies):
+        for copy in copies:
+            copy.wait_recv()
+
+    def own(j, c, device):
+        return remote(mean.at[c, :, part(j)], cols.at[group, c, :, part(j)], device)
+
+    def relay(j, c, origin, device):
+        piece = cols.at[origin, c, :, part(j)]
+        return remote(piece, piece, device)
+
+    y_own = [[own(j, c, across_y) for c in range(2)] for j in range(chunks)]
+    z_own = [[own(j, c, across_z) for c in range(2)] for j in range(chunks)]
+    relays = [
+        [
+            relay(j, 0, group_y, across_z) if 2 * j < chunks else relay(j, 0, group_z, across_y),
+            relay(j, 1, group_z, across_y),
+        ]
+        for j in range(chunks)
     ]
-    relays = [
-        send(6, cols.at[group_y, 0], cols.at[group_y, 0], across_z),
-        send(7, cols.at[group_z, 1], cols.at[group_z, 1], across_y),
-        send(8, rows.at[recv_x], rows.at[recv_x], across_core),
+    row_x = [remote(mean.at[:, half(f)], rows.at[mine, :, half(f)], across_x) for f in range(2)]
+    row_core = [remote(mean.at[:, half(f)], rows.at[mine, :, half(f)], across_core) for f in range(2)]
+    row_relay = [
+        remote(rows.at[recv_x, :, half(f)], rows.at[recv_x, :, half(f)], across_core)
+        for f in range(2)
     ]
+    homes = [
+        remote(home.at[:, :, part(j)], got.at[:, :, part(j)], partner) for j in range(chunks)
+    ]
+
+    def send_own(j):
+        start(y_own[j][0], z_own[j][1], z_own[j][0], y_own[j][1])
+
+    send_own(0)
+    start(row_x[0], row_core[0])
     locals_ = [
-        pltpu.make_async_copy(mean, cols.at[group], local_sems.at[0]),
-        pltpu.make_async_copy(mean, rows.at[mine], local_sems.at[1]),
+        pltpu.make_async_copy(mean, rows.at[mine], local_sems.at[0]),
+        pltpu.make_async_copy(mean, cols.at[group], local_sems.at[1]),
     ]
-    for copy in copies + locals_:
+    for copy in locals_:
         copy.start()
-    for copy, relay in zip(copies, relays):
-        copy.wait_recv()
-        relay.start()
-    for copy in copies[3:] + relays:
-        copy.wait_recv()
-    for copy in copies + relays:
+    start(row_x[1], row_core[1])
+
+    def multiply(flip, columns):
+        acc[...] = jnp.zeros_like(acc)
+
+        @pl.loop(0, 4)
+        def _(r):
+            for y in range(2):
+                left = rows.at[r, :, half(flip), pl.ds(y * size, size)]
+                depth = pl.ds(pl.multiple_of((r // 2) * size, size), size)
+                right = cols.at[(r % 2) * 2 + y, :, depth, columns]
+                dot = functools.partial(jnp.dot, preferred_element_type=jnp.float32)
+                acc[0] += dot(left[0], right[0]) - dot(left[1], right[1])
+                acc[1] += dot(left[0], right[1]) + dot(left[1], right[0])
+
+    def keep(first, last):
+        @pl.loop(first, last)
+        def _(j):
+            columns = pl.ds(pl.multiple_of(j * wide, wide), wide)
+            multiply(1, columns)
+            kept[:, :, columns] = acc[...] * scale
+
+    for j in range(chunks):
+        first_relay, second_relay = relays[j]
+        if 2 * j < chunks:
+            arrive(y_own[j][0])
+            start(first_relay)
+            arrive(z_own[j][1])
+            start(second_relay)
+            rest = [y_own[j][1], z_own[j][0]]
+        else:
+            arrive(z_own[j][1])
+            start(second_relay)
+            arrive(z_own[j][0])
+            start(first_relay)
+            rest = y_own[j]
+        if j + 1 < chunks:
+            send_own(j + 1)
+        if j == 0:
+            arrive(row_x[0])
+            start(row_relay[0])
+            for copy in locals_:
+                copy.wait()
+            arrive(row_core[0])
+        if j == chunks // 2:
+            arrive(row_x[1])
+            start(row_relay[1])
+            arrive(row_core[1])
+        arrive(*rest)
+        arrive(first_relay, second_relay)
+        if j == 0:
+            arrive(row_relay[0])
+        multiply(0, part(j))
+        home[:, :, part(j)] = (acc[...] * scale).astype(home.dtype)
+        start(homes[j])
+        if j == chunks // 2:
+            arrive(row_relay[1])
+            keep(0, j)
+    keep(chunks // 2, chunks)
+    arrive(*homes)
+    for copy in started:
         copy.wait_send()
-    for copy in locals_:
-        copy.wait()
-
-
-def gather(mean):
-    panel = jax.ShapeDtypeStruct((4,) + mean.shape, mean.dtype)
+
+
+def multiply(mean, chunks=4):
+    height, width = mean.shape[1:]
+    size = height // 2
+    copies = 7 * chunks + 6
     return pl.pallas_call(
-        gather_kernel,
-        out_shape=(panel, panel),
+        functools.partial(multiply_kernel, chunks, float(NS) ** (-0.5)),
+        out_shape=(
+            jax.ShapeDtypeStruct((2, size, width), jnp.float32),
+            jax.ShapeDtypeStruct((2, size, width), mean.dtype),
+        ),
         in_specs=[ANY],
-        out_specs=(ANY, ANY),
+        out_specs=(pl.BlockSpec(memory_space=pltpu.VMEM), ANY),
         scratch_shapes=[
+            pltpu.VMEM((4,) + mean.shape, mean.dtype),
+            pltpu.VMEM((4,) + mean.shape, mean.dtype),
+            pltpu.VMEM((2, size, width), mean.dtype),
+            pltpu.VMEM((2, size, width // chunks), jnp.float32),
             pltpu.SemaphoreType.DMA((2,)),
-            pltpu.SemaphoreType.DMA((9,)),
-            pltpu.SemaphoreType.DMA((9,)),
+            pltpu.SemaphoreType.DMA((copies,)),
+            pltpu.SemaphoreType.DMA((copies,)),
         ],
-        compiler_params=pltpu.CompilerParams(collective_id=1, has_side_effects=True),
-        name="gather",
+        compiler_params=pltpu.CompilerParams(
+            collective_id=1, has_side_effects=True, vmem_limit_bytes=52 * 2**20
+        ),
+        cost_estimate=pl.CostEstimate(
+            flops=2 * 4 * height * width * 4 * width, bytes_accessed=16 * 2**20, transcendentals=0
+        ),
+        name="multiply",
     )(mean)
 
 
-def product_kernel(scale, rows, cols, out):
-    half = rows.shape[2] // 2
-    real = imag = None
-    for k in range(8):
-        left = rows.at[k // 2, :, :, pl.ds((k % 2) * half, half)]
-        right = cols.at[k % 4, :, pl.ds((k // 4) * half, half), :]
-        dot = functools.partial(jnp.dot, preferred_element_type=jnp.float32)
-        re = dot(left[0], right[0]) - dot(left[1], right[1])
-        im = dot(left[0], right[1]) + dot(left[1], right[0])
-        real, imag = (re, im) if real is None else (real + re, imag + im)
-    out[0] = real * scale
-    out[1] = imag * scale
-
-
-def product(rows, cols, tile_cols=256):
-    size = rows.shape[2]
-    return pl.pallas_call(
-        functools.partial(product_kernel, float(NS) ** (-0.5)),
-        grid=(size // tile_cols,),
-        out_shape=jax.ShapeDtypeStruct((2, size, size), jnp.float32),
-        in_specs=[
-            pl.BlockSpec(rows.shape, lambda n: (0, 0, 0, 0), pipeline_mode=pl.Buffered(1)),
-            pl.BlockSpec((4, 2, size, tile_cols), lambda n: (0, 0, 0, n)),
-        ],
-        out_specs=pl.BlockSpec((2, size, tile_cols), lambda n: (0, 0, n)),
-        compiler_params=pltpu.CompilerParams(vmem_limit_bytes=56 * 2**20),
-        cost_estimate=pl.CostEstimate(
-            flops=2 * 4 * size * size * 4 * size, bytes_accessed=40 * 2**20, transcendentals=0
-        ),
-        name="product",
-    )(rows, cols)
-
-
 def cube_per_device(traces):
-    size = traces.shape[2]
-    hi = lax.axis_index("shot") // 4
-    mean = average(*exchange(traces))
-    result = product(*gather(mean)).reshape(2, 2, size, 2 * size)
-    kept = lax.dynamic_index_in_dim(result, hi, 1, keepdims=False)
-    sent = lax.dynamic_index_in_dim(result, 1 - hi, 1, keepdims=False).astype(jnp.bfloat16)
-    got = lax.ppermute(sent, "shot", [(s, (s + 4) % 8) for s in range(8)]).astype(jnp.float32)
-    first = hi == 0
+    kept, got = multiply(average(*exchange(traces)))
+    first = lax.axis_index("shot") // 4 == 0
+    got = got.astype(jnp.float32)
     return jnp.stack((jnp.where(first, kept, got), jnp.where(first, got, kept)))
 
 

time: 536 us -> 335 us (0.62); the launches traced: 530 us -> 335 us
  Pallas kernels: 419 us -> 320 us
  waiting for transfers between devices: 91.6 us -> 0 us
    pallas_call x2 -> x1, Pallas kernels: 305 us -> 207 us  [multiply(): pl.pallas_call(functools.partial(multiply_kernel, chunks, float(NS) ** (-...]
    ppermute x1 -> x0, waiting for transfers between devices: 91.6 us -> none  [cube_per_device(): lax.ppermute(sent, 'shot', [(s, (s + 4) % 8) for s in range(8)])]
  transfers between devices with their start and end apart: 1 -> 0, of which waited for: 1 -> 0; matrix products, arithmetic and copies ran while one was open for 0% -> 0% of each run, Pallas kernels for 0% -> 0%
where the time goes in v2:
time: 335 us
  Pallas kernels  320 us (96%)
  other arithmetic  8.28 us (2%)
  local copies, waits for them, and re-layouts  6.38 us (2%)
    pallas_call x1, Pallas kernels, multiply(): pl.pallas_call(functools.partial(multiply_kernel, chunks, float(NS) ** (-...  207 us
    pallas_call x1, Pallas kernels, exchange(): pl.pallas_call(exchange_kernel, out_shape=(jax.ShapeDtypeStruct((2, 2, si...  111 us
    another operation x2, other arithmetic, cube_per_device(): return jnp.stack((jnp.where(first, kept, got), jnp.where(first, got, kept)))  8.28 us

profile of v2, /device:TPU:24, one launch (start us, length us, event | category | flops | bytes accessed | tf_op | source)
XLA Modules:
  0.0 334.8 jit_solution(8584444136965394981)
XLA Ops:
  0.0 110.9 %exchange.1 = (bf16[2,2,512,1024]{3,2,1,0:T(8,128)(2,1)}, bf16[2,2,2,512,512]{4,3,2,1,0:T(8,128)(2,1)}) custom-call(bf16[2,2,512,1024]{3,2,1,0:T(8,128)(2,1)} %traces.1), custom_call_target="tpu_custom_call" | custom-call | tf_op jit(solution)/shard_map/exchange/pallas_call | solution.py:127
  110.9 0.0 copy-start.1
  110.9 2.2 copy-done.1
  113.0 0.0 copy-start.2
  113.1 2.2 copy-done.2
  115.2 2.6 average.1.mean
  117.8 0.0 copy-start
  117.8 2.0 copy-done
  119.8 206.7 %multiply.1 = (f32[2,512,1024]{2,1,0:T(8,128)}, bf16[2,512,1024]{2,1,0:T(8,128)(2,1)}) custom-call(bf16[2,1024,1024]{2,1,0:T(8,128)(2,1)} %copy-done), custom_call_target="tpu_custom_call" | custom-call | flops 34359738368 | bytes 16777216 | tf_op jit(solution)/shard_map/multiply/pallas_call | solution.py:312
  326.5 4.0 %fusion = (f32[1,2,512,1024]{3,2,1,0:T(8,128)S(1)}, f32[1,2,512,1024]{3,2,1,0:T(8,128)S(1)}) fusion(f32[2,512,1024]{2,1,0:T(8,128)} %get-tuple-element.11, bf16[2,512,1024]{2,1,0:T(8,128)(2,1)} %get-tuple-element.12, pred[]{:T(512)S(6)} %eq.3), kind=kLoop, calls=%fused_computation.3 | loop fusion | flops 3145728 | bytes 14680065 | tf_op jit(solution)/shard_map/stack | solution.py:343
  330.6 4.2 %pad_maximum_fusion = f32[2,2,512,1024]{3,2,1,0:T(8,128)} fusion(f32[1,2,512,1024]{3,2,1,0:T(8,128)S(1)} %get-tuple-element.14, f32[1,2,512,1024]{3,2,1,0:T(8,128)S(1)} %get-tuple-element.13), kind=kLoop, calls=%fused_computation | loop fusion | flops 2097152 | bytes 16777216 | tf_op jit(solution)/shard_map/stack | solution.py:343
Async XLA Ops:
  110.9 2.2 copy-start.1
  113.0 2.2 copy-start.2
  117.8 2.0 copy-start

commit v3 on v2

--- a/solution.py
+++ b/solution.py
@@ -36,6 +36,11 @@
 def exchange_kernel(traces, tile, mirror, local_sems, swap_sems, send_sems, recv_sems):
     me = Place()
     size = traces.shape[2]
+    pieces = 4
+
+    def at(i):
+        return i // 2, pl.ds((i % 2) * (size // 2), size // 2)
+
     partner = me.device(hi=1 - me.hi)
     blocks = [(flip, col) for flip in range(2) for col in range(2)]
 
@@ -59,11 +64,11 @@
 
     swaps = [
         pltpu.make_async_remote_copy(
-            src_ref=traces.at[1 - me.hi, c], dst_ref=tile.at[c, me.hi],
+            src_ref=traces.at[(1 - me.hi, *at(c))], dst_ref=tile.at[at(c)[0], me.hi, at(c)[1]],
             send_sem=swap_sems.at[0, c], recv_sem=swap_sems.at[1, c],
             device_id=partner, device_id_type=MESH,
         )
-        for c in range(2)
+        for c in range(pieces)
     ]
     for swap in swaps:
         swap.start()
@@ -73,19 +78,19 @@
     def source(flip, col, c):
         columns = pl.ds(col * size, size)
         if flip == 0:
-            return traces.at[me.hi, c, :, columns]
-        return tile.at[c, 1 - me.hi, :, columns]
+            return traces.at[(me.hi, *at(c), columns)]
+        return tile.at[at(c)[0], 1 - me.hi, at(c)[1], columns]
 
     def remote(flip, col, c):
         return pltpu.make_async_remote_copy(
-            src_ref=source(flip, col, c), dst_ref=mirror.at[c, me.x, me.y],
+            src_ref=source(flip, col, c), dst_ref=mirror.at[at(c)[0], me.x, me.y, at(c)[1]],
             send_sem=send_sems.at[c, half(flip), col], recv_sem=recv_sems.at[c, me.x, me.y],
             device_id=target(flip, col), device_id_type=MESH,
         )
 
     def local(flip, col, c):
         return pltpu.make_async_copy(
-            source(flip, col, c), mirror.at[c, me.x, me.y], local_sems.at[1 + c]
+            source(flip, col, c), mirror.at[at(c)[0], me.x, me.y, at(c)[1]], local_sems.at[1 + c]
         )
 
     def begin(flip, c):
@@ -98,13 +103,13 @@
             def _():
                 remote(flip, col, c).start()
 
-    for c in range(2):
+    for c in range(pieces):
         begin(0, c)
-    for c in range(2):
+    for c in range(pieces):
         swaps[c].wait_recv()
         begin(1, c)
     own.wait()
-    for c in range(2):
+    for c in range(pieces):
         swaps[c].wait_send()
         for flip, col in blocks:
             @pl.when(is_self(flip, col))
@@ -115,7 +120,7 @@
             def _():
                 remote(flip, col, c).wait_send()
                 pltpu.make_async_remote_copy(
-                    src_ref=mirror.at[c, half(flip), col], dst_ref=mirror.at[c, half(flip), col],
+                    src_ref=mirror.at[at(c)[0], half(flip), col, at(c)[1]], dst_ref=mirror.at[at(c)[0], half(flip), col, at(c)[1]],
                     send_sem=send_sems.at[c, half(flip), col],
                     recv_sem=recv_sems.at[c, half(flip), col],
                     device_id=target(flip, col), device_id_type=MESH,
@@ -133,10 +138,10 @@
         in_specs=[ANY],
         out_specs=(ANY, ANY),
         scratch_shapes=[
-            pltpu.SemaphoreType.DMA((3,)),
-            pltpu.SemaphoreType.DMA((2, 2)),
-            pltpu.SemaphoreType.DMA((2, 2, 2)),
-            pltpu.SemaphoreType.DMA((2, 2, 2)),
+            pltpu.SemaphoreType.DMA((5,)),
+            pltpu.SemaphoreType.DMA((2, 4)),
+            pltpu.SemaphoreType.DMA((4, 2, 2)),
+            pltpu.SemaphoreType.DMA((4, 2, 2)),
         ],
         compiler_params=pltpu.CompilerParams(collective_id=0, has_side_effects=True),
         name="exchange",

time: 335 us -> 321 us (0.958)
  Pallas kernels: 320 us -> 306 us
    pallas_call x1, Pallas kernels: 111 us -> 102 us  [exchange(): pl.pallas_call(exchange_kernel, out_shape=(jax.ShapeDtypeStruct((2, 2, si...]
    pallas_call x1, Pallas kernels: 207 us -> 202 us  [multiply(): pl.pallas_call(functools.partial(multiply_kernel, chunks, float(NS) ** (-...]
where the time goes in v3:
time: 321 us
  Pallas kernels  306 us (95%)
  other arithmetic  8.28 us (3%)
  local copies, waits for them, and re-layouts  6.38 us (2%)
    pallas_call x1, Pallas kernels, multiply(): pl.pallas_call(functools.partial(multiply_kernel, chunks, float(NS) ** (-...  202 us
    pallas_call x1, Pallas kernels, exchange(): pl.pallas_call(exchange_kernel, out_shape=(jax.ShapeDtypeStruct((2, 2, si...  102 us
    another operation x2, other arithmetic, cube_per_device(): return jnp.stack((jnp.where(first, kept, got), jnp.where(first, got, kept)))  8.28 us

profile of v3, /device:TPU:24, one launch (start us, length us, event | category | flops | bytes accessed | tf_op | source)
XLA Modules:
  0.0 321.1 jit_solution(1852707108185430207)
XLA Ops:
  0.0 101.9 %exchange.1 = (bf16[2,2,512,1024]{3,2,1,0:T(8,128)(2,1)}, bf16[2,2,2,512,512]{4,3,2,1,0:T(8,128)(2,1)}) custom-call(bf16[2,2,512,1024]{3,2,1,0:T(8,128)(2,1)} %traces.1), custom_call_target="tpu_custom_call" | custom-call | tf_op jit(solution)/shard_map/exchange/pallas_call | solution.py:132
  101.9 0.0 copy-start.1
  101.9 2.2 copy-done.1
  104.1 0.0 copy-start.2
  104.1 2.2 copy-done.2
  106.3 2.6 average.1.mean
  108.9 0.0 copy-start
  108.9 2.0 copy-done
  110.9 201.9 %multiply.1 = (f32[2,512,1024]{2,1,0:T(8,128)}, bf16[2,512,1024]{2,1,0:T(8,128)(2,1)}) custom-call(bf16[2,1024,1024]{2,1,0:T(8,128)(2,1)} %copy-done), custom_call_target="tpu_custom_call" | custom-call | flops 34359738368 | bytes 16777216 | tf_op jit(solution)/shard_map/multiply/pallas_call | solution.py:317
  312.8 4.0 %fusion = (f32[1,2,512,1024]{3,2,1,0:T(8,128)S(1)}, f32[1,2,512,1024]{3,2,1,0:T(8,128)S(1)}) fusion(f32[2,512,1024]{2,1,0:T(8,128)} %get-tuple-element.11, bf16[2,512,1024]{2,1,0:T(8,128)(2,1)} %get-tuple-element.12, pred[]{:T(512)S(6)} %eq.3), kind=kLoop, calls=%fused_computation.3 | loop fusion | flops 3145728 | bytes 14680065 | tf_op jit(solution)/shard_map/stack | solution.py:348
  316.8 4.2 %pad_maximum_fusion = f32[2,2,512,1024]{3,2,1,0:T(8,128)} fusion(f32[1,2,512,1024]{3,2,1,0:T(8,128)S(1)} %get-tuple-element.14, f32[1,2,512,1024]{3,2,1,0:T(8,128)S(1)} %get-tuple-element.13), kind=kLoop, calls=%fused_computation | loop fusion | flops 2097152 | bytes 16777216 | tf_op jit(solution)/shard_map/stack | solution.py:348
Async XLA Ops:
  101.9 2.2 copy-start.1
  104.1 2.2 copy-start.2
  108.9 2.0 copy-start
